TPU v7x, 512 devices: a whole 4x8x8 slice. The times are simulated.
512 devices in a mesh: blk: 512 (over x, z, y, core).
Axes of the slice: x: 4, y: 8, z: 8, core: 2. Of those that a mesh axis runs over, the one named last changes fastest.
Arguments:
- users: float32 [524288, 128], P('blk'), may hold values from -4 to 4
- user_bias: float32 [524288], P('blk'), may hold values from -6 to 6
- items: float32 [262144, 128], P('blk'), may hold values from -4 to 4
- item_bias: float32 [262144], P('blk'), may hold values from -6 to 6
- global_mean: float32 [], replicated, may hold values from 2 to 4
- item_owner: int32 [2, 512], P(None, 'blk'), may hold values from 0 to 511, as said below
- tile_rows: int32 [2, 512, 16], P(None, 'blk'), may hold values from 0 to 7
- tile_cols: int32 [2, 512, 16], P(None, 'blk'), may hold values from 0 to 3
- tile_counts: int32 [2, 512], P(None, 'blk'), may hold values from 1 to 16, as said below
- ratings: bfloat16 [2, 512, 16, 128, 128], P(None, 'blk'), may hold values from 1 to 5
- observed: int32 [2, 512, 16, 128, 128], P(None, 'blk'), may hold values 0 or 1
Outputs:
- users_out: float32 [524288, 128], P('blk')
- user_bias_out: float32 [524288], P('blk')
- items_out: float32 [262144, 128], P('blk')
- item_bias_out: float32 [262144], P('blk')
- mean_out: float32 [], replicated
Inputs may be any that keep to these rules, and one draw needn't show every extreme that they name: For each s there is a number m_s with item_owner[s, b] = b XOR m_s for every b; every bit of a block index is set in some m_s. `tile_counts`: in each sub-epoch some block pair uses all 16 slots.
All inputs are finite; a program needn't handle non-finite values. No bound on the sum of `observed` on one device may be relied on, other than what follows from the above.
Results may differ from a plain program's by a relative error of at most 0.0018.
Values sent between devices are 32-bit elements; how exact they have to be, the bound alone decides.
A program may use at most 64 MiB of HBM per device.

v0:
```python
import jax
import jax.numpy as jnp
from jax import lax
from jax.sharding import PartitionSpec as P

SUBEP = 2


step_scale = 0.8
bias_rate = 0.005
shrink = 0.02
mean_rate = 0.5


def from_partner(block, axis, apart):
    count = lax.axis_size(axis)
    route = []
    for low in range(count):
        high = low | 1 << apart
        if high != low and high < count:
            route += [(low, high), (high, low)]
    return lax.ppermute(block, axis, route)


def tile_step(t, carry, mean, rows, cols, count, ratings, observed):
    users, ubias, items, ibias, err_sum, obs_sum = carry
    edge = ratings.shape[-1]
    rank = users.shape[1]
    learn_rate = step_scale / edge
    row0 = rows[t] * edge
    col0 = cols[t] * edge
    zero = jnp.int32(0)
    u = lax.dynamic_slice(users, (row0, zero), (edge, rank))
    v = lax.dynamic_slice(items, (col0, zero), (edge, rank))
    bu = lax.dynamic_slice_in_dim(ubias, row0, edge)
    bv = lax.dynamic_slice_in_dim(ibias, col0, edge)
    uh = u.astype(jnp.bfloat16)
    vh = v.astype(jnp.bfloat16)
    score = lax.dot_general(uh, vh, (((1,), (1,)), ((), ())), preferred_element_type=jnp.float32)
    obs = observed[t].astype(jnp.float32)
    err = obs * (ratings[t].astype(jnp.float32) - (mean + bu[:, None] + bv[None, :] + score))
    eh = err.astype(jnp.bfloat16)
    grad_u = jnp.dot(eh, vh, preferred_element_type=jnp.float32)
    grad_v = lax.dot_general(eh, uh, (((0,), (0,)), ((), ())), preferred_element_type=jnp.float32)
    active = t < count
    new_u = jnp.where(active, u + learn_rate * (grad_u - shrink * u), u)
    new_v = jnp.where(active, v + learn_rate * (grad_v - shrink * v), v)
    new_bu = jnp.where(active, bu + bias_rate * (jnp.sum(err, axis=1) - shrink * bu), bu)
    new_bv = jnp.where(active, bv + bias_rate * (jnp.sum(err, axis=0) - shrink * bv), bv)
    users = lax.dynamic_update_slice(users, new_u, (row0, zero))
    items = lax.dynamic_update_slice(items, new_v, (col0, zero))
    ubias = lax.dynamic_update_slice_in_dim(ubias, new_bu, row0, 0)
    ibias = lax.dynamic_update_slice_in_dim(ibias, new_bv, col0, 0)
    err_sum = err_sum + jnp.where(active, jnp.sum(err), jnp.float32(0.0))
    obs_sum = obs_sum + jnp.where(active, jnp.sum(obs), jnp.float32(0.0))
    return (users, ubias, items, ibias, err_sum, obs_sum)


def bit_taken(relative, bit):
    return jnp.bitwise_and(jnp.right_shift(relative, bit), 1) == 1


def hop_plain(bit, relative, items, item_bias):
    far_items, far_bias = from_partner((items, item_bias), "blk", bit)
    take = bit_taken(relative, bit)
    return (jnp.where(take, far_items, items), jnp.where(take, far_bias, item_bias))


def on_device(
    users,
    user_bias,
    items,
    item_bias,
    global_mean,
    item_owner,
    tile_rows,
    tile_cols,
    tile_counts,
    ratings,
    observed,
):
    index = lax.axis_index("blk")
    nbits = lax.axis_size("blk").bit_length() - 1
    masks = jnp.bitwise_xor(item_owner[:, 0], index)
    bit_list = list(range(nbits))
    mean = global_mean
    for section in range(SUBEP + 1):
        if section == 0:
            relative = masks[0]
        elif section == SUBEP:
            relative = masks[SUBEP - 1]
        else:
            relative = jnp.bitwise_xor(masks[section], masks[section - 1])
        for bit in bit_list:
            items, item_bias = hop_plain(bit, relative, items, item_bias)
        if section < SUBEP:
            rows = tile_rows[section, 0]
            cols = tile_cols[section, 0]
            count = tile_counts[section, 0]
            tiles = ratings[section, 0]
            seen = observed[section, 0]

            def advance(t, carry):
                return tile_step(t, carry, mean, rows, cols, count, tiles, seen)

            init = (users, user_bias, items, item_bias, jnp.float32(0.0), jnp.float32(0.0))
            result = lax.fori_loop(0, rows.shape[0], advance, init)
            users, user_bias, items, item_bias, err_sum, obs_sum = result
            total_err, total_obs = lax.psum((err_sum, obs_sum), "blk")
            mean = mean + mean_rate * total_err / total_obs
    return (users, user_bias, items, item_bias, mean)


def solution(mesh):
    in_specs = (
        P("blk", None),
        P("blk"),
        P("blk", None),
        P("blk"),
        P(),
        P(None, "blk"),
        P(None, "blk", None),
        P(None, "blk", None),
        P(None, "blk"),
        P(None, "blk", None, None, None),
        P(None, "blk", None, None, None),
    )
    out_specs = (P("blk", None), P("blk"), P("blk", None), P("blk"), P())
    return jax.shard_map(
        on_device, mesh=mesh, in_specs=in_specs, out_specs=out_specs, check_vma=False
    )
```

profile of v0, /device:TPU:1, one launch (start us, length us, event | category | flops | bytes accessed | tf_op | source)
XLA Modules:
  0.0 809.8 jit_solution(16369416096196414051)
XLA Ops:
  0.7 8.9 %collective-permute-start = (f32[512,128]{1,0:T(8,128)}, f32[512,128]{1,0:T(8,128)S(1)}, u32[]{:S(2)}, u32[]{:S(2)}) collective-permute-start(f32[512,128]{1,0:T(8,128)} %param.17), channel_id=1, source_target_pairs={{0,1},{1,0},{2,3},{3,2},{4,5},{5,4},{6,7},{7,6},{8,9},{9,8},{10,11... | collective-permute-start | bytes 786440 | tf_op jit(solution)/shard_map/ppermute | solution.py:22
  14.1 7.2 collective-permute-done.1
  28.8 9.2 %collective-permute-done.2 = f32[512,128]{1,0:T(8,128)S(1)} collective-permute-done((f32[512,128]{1,0:T(8,128)S(1)}, f32[512,128]{1,0:T(8,128)S(1)}, u32[]{:S(2)}, u32[]{:S(2)}) %collective-permute-start.2) | collective-permute-done | bytes 262176 | tf_op jit(solution)/shard_map/ppermute | solution.py:22
  42.6 5.5 collective-permute-done.11
  48.1 7.0 collective-permute-start.12
  71.6 8.0 collective-permute-start.15
  83.0 8.1 %collective-permute-start.6 = (f32[512,128]{1,0:T(8,128)S(1)}, f32[512,128]{1,0:T(8,128)S(1)}, u32[]{:S(2)}, u32[]{:S(2)}) collective-permute-start(f32[512,128]{1,0:T(8,128)S(1)} %broadcast_select_fusion.27), channel_id=1, source_target_pairs={{0,64},{64,0},{1,65},{65,1},{2,66},{66,2},{3,67},{67,3},{4,68},{68... | collective-permute-start | bytes 786440 | tf_op jit(solution)/shard_map/ppermute | solution.py:22
  102.8 4.4 collective-permute-start.17
  112.0 4.6 collective-permute-done.8
  116.7 145.7 %while.46 = (s32[]{:T(128)}, f32[1024,128]{1,0:T(8,128)S(1)}, f32[1024]{0:T(1024)S(1)}, f32[512,128]{1,0:T(8,128)S(1)}, f32[512]{0:T(512)S(1)}, /*index=5*/f32[]...) while((s32[]{:T(128)}, f32[1024,128]{1,0:T(8,128)S(1)}, ...), condition=%wide.region_5.6_spmd, body=%wide.region_0.5_spmd.sunk | while | flops 12944525 | bytes 1711515 | solution.py:107
  262.4 7.9 collective-permute-start.18
  271.6 6.9 collective-permute-start.19
  278.5 6.5 collective-permute-done.19
  287.1 13.8 %collective-permute-done.20 = f32[512,128]{1,0:T(8,128)S(1)} collective-permute-done((f32[512,128]{1,0:T(8,128)S(1)}, f32[512,128]{1,0:T(8,128)S(1)}, u32[]{:S(2)}, u32[]{:S(2)}) %collective-permute-start.20) | collective-permute-done | bytes 262176 | tf_op jit(solution)/shard_map/ppermute | solution.py:22
  300.9 4.7 collective-permute-start.21
  305.7 14.6 %collective-permute-done.21 = f32[512,128]{1,0:T(8,128)S(1)} collective-permute-done((f32[512,128]{1,0:T(8,128)S(1)}, f32[512,128]{1,0:T(8,128)S(1)}, u32[]{:S(2)}, u32[]{:S(2)}) %collective-permute-start.21) | collective-permute-done | bytes 262176 | tf_op jit(solution)/shard_map/ppermute | solution.py:22
  331.9 5.3 collective-permute-start.29
  346.3 4.5 collective-permute-start.24
  352.7 9.4 %collective-permute-done.31 = f32[512]{0:T(512)S(1)} collective-permute-done((f32[512]{0:T(512)S(1)}, f32[512]{0:T(512)S(1)}, u32[]{:S(2)}, u32[]{:S(2)}) %collective-permute-start.31) | collective-permute-done | bytes 2080 | tf_op jit(solution)/shard_map/ppermute | solution.py:22
  368.1 4.7 collective-permute-start.33
  386.5 100.9 %all-reduce.1 = (f32[]{:T(128)}, f32[]{:T(128)}) all-reduce(f32[]{:T(128)} %get-tuple-element.447, f32[]{:T(128)} %get-tuple-element.448), channel_id=1, replica_groups=mesh['blk'=512] {'blk'}, use_global_device_ids=true, to_apply=%region_6.7 | all-reduce | flops 2 | bytes 16 | tf_op jit(solution)/shard_map/psum | solution.py:109
  488.7 105.1 %while.47 = (s32[]{:T(128)}, f32[1024,128]{1,0:T(8,128)S(1)}, f32[1024]{0:T(1024)S(1)}, f32[512,128]{1,0:T(8,128)S(1)}, f32[512]{0:T(512)S(1)}, /*index=5*/f32[]...) while((s32[]{:T(128)}, f32[1024,128]{1,0:T(8,128)S(1)}, ...), condition=%wide.region_13.14_spmd, body=%wide.region_8.13_spmd.sunk | while | flops 12944525 | bytes 1711515 | solution.py:107
  600.2 6.8 collective-permute-done.37
  610.8 12.8 %collective-permute-done.38 = f32[512,128]{1,0:T(8,128)S(1)} collective-permute-done((f32[512,128]{1,0:T(8,128)S(1)}, f32[512,128]{1,0:T(8,128)S(1)}, u32[]{:S(2)}, u32[]{:S(2)}) %collective-permute-start.38) | collective-permute-done | bytes 262176 | tf_op jit(solution)/shard_map/ppermute | solution.py:22
  623.7 5.8 collective-permute-start.39
  630.1 12.5 %collective-permute-done.39 = f32[512,128]{1,0:T(8,128)S(1)} collective-permute-done((f32[512,128]{1,0:T(8,128)S(1)}, f32[512,128]{1,0:T(8,128)S(1)}, u32[]{:S(2)}, u32[]{:S(2)}) %collective-permute-start.39) | collective-permute-done | bytes 262176 | tf_op jit(solution)/shard_map/ppermute | solution.py:22
  658.4 5.8 collective-permute-start.48
  666.9 4.4 collective-permute-start.42
  673.8 8.5 %collective-permute-done.49 = f32[512]{0:T(512)S(1)} collective-permute-done((f32[512]{0:T(512)S(1)}, f32[512]{0:T(512)S(1)}, u32[]{:S(2)}, u32[]{:S(2)}) %collective-permute-start.49) | collective-permute-done | bytes 2080 | tf_op jit(solution)/shard_map/ppermute | solution.py:22
  682.4 4.8 collective-permute-start.50
  689.6 4.6 collective-permute-start.51
  708.3 97.6 %all-reduce = (f32[]{:T(128)}, f32[]{:T(128)}) all-reduce(f32[]{:T(128)} %get-tuple-element.453, f32[]{:T(128)} %get-tuple-element.454), channel_id=1, replica_groups=mesh['blk'=512] {'blk'}, use_global_device_ids=true, to_apply=%region_14.15 | all-reduce | flops 2 | bytes 16 | tf_op jit(solution)/shard_map/psum | solution.py:109
  (512 shorter events, 278.6 us)
Async XLA Ops:
  0.7 10.8 %collective-permute-start = (f32[512,128]{1,0:T(8,128)}, f32[512,128]{1,0:T(8,128)S(1)}, u32[]{:S(2)}, u32[]{:S(2)}) collective-permute-start(f32[512,128]{1,0:T(8,128)} %param.17), channel_id=1, source_target_pairs={{0,1},{1,0},{2,3},{3,2},{4,5},{5,4},{6,7},{7,6},{8,9},{9,8},{10,11... | collective-permute-start | bytes 786440 | tf_op jit(solution)/shard_map/ppermute | solution.py:22
  11.5 9.8 %collective-permute-start.1 = (f32[512,128]{1,0:T(8,128)S(1)}, f32[512,128]{1,0:T(8,128)S(1)}, u32[]{:S(2)}, u32[]{:S(2)}) collective-permute-start(f32[512,128]{1,0:T(8,128)S(1)} %broadcast_select_fusion.22), channel_id=1, source_target_pairs={{0,2},{2,0},{1,3},{3,1},{4,6},{6,4},{5,7},{7,5},{8,10},{10,8},{9,1... | collective-permute-start | bytes 786440 | tf_op jit(solution)/shard_map/ppermute | solution.py:22
  21.4 16.6 %collective-permute-start.2 = (f32[512,128]{1,0:T(8,128)S(1)}, f32[512,128]{1,0:T(8,128)S(1)}, u32[]{:S(2)}, u32[]{:S(2)}) collective-permute-start(f32[512,128]{1,0:T(8,128)S(1)} %broadcast_select_fusion.23), channel_id=1, source_target_pairs={{0,4},{4,0},{1,5},{5,1},{2,6},{6,2},{3,7},{7,3},{8,12},{12,8},{9,1... | collective-permute-start | bytes 786440 | tf_op jit(solution)/shard_map/ppermute | solution.py:22
  26.8 13.2 %collective-permute-start.10 = (f32[512]{0:T(512)S(1)}, f32[512]{0:T(512)S(1)}, u32[]{:S(2)}, u32[]{:S(2)}) collective-permute-start(f32[512]{0:T(512)S(1)} %broadcast_select_fusion.49), channel_id=1, source_target_pairs={{0,2},{2,0},{1,3},{3,1},{4,6},{6,4},{5,7},{7,5},{8,10},{10,8},{9,1... | collective-permute-start | bytes 6152 | tf_op jit(solution)/shard_map/ppermute | solution.py:22
  38.0 17.1 %collective-permute-start.3 = (f32[512,128]{1,0:T(8,128)S(1)}, f32[512,128]{1,0:T(8,128)S(1)}, u32[]{:S(2)}, u32[]{:S(2)}) collective-permute-start(f32[512,128]{1,0:T(8,128)S(1)} %broadcast_select_fusion.24), channel_id=1, source_target_pairs={{0,8},{8,0},{1,9},{9,1},{2,10},{10,2},{3,11},{11,3},{4,12},{12,4},... | collective-permute-start | bytes 786440 | tf_op jit(solution)/shard_map/ppermute | solution.py:22
  55.2 12.0 %collective-permute-start.4 = (f32[512,128]{1,0:T(8,128)S(1)}, f32[512,128]{1,0:T(8,128)S(1)}, u32[]{:S(2)}, u32[]{:S(2)}) collective-permute-start(f32[512,128]{1,0:T(8,128)S(1)} %broadcast_select_fusion.25), channel_id=1, source_target_pairs={{0,16},{16,0},{1,17},{17,1},{2,18},{18,2},{3,19},{19,3},{4,20},{20... | collective-permute-start | bytes 786440 | tf_op jit(solution)/shard_map/ppermute | solution.py:22
  67.2 15.7 %collective-permute-start.5 = (f32[512,128]{1,0:T(8,128)S(1)}, f32[512,128]{1,0:T(8,128)S(1)}, u32[]{:S(2)}, u32[]{:S(2)}) collective-permute-start(f32[512,128]{1,0:T(8,128)S(1)} %broadcast_select_fusion.26), channel_id=1, source_target_pairs={{0,32},{32,0},{1,33},{33,1},{2,34},{34,2},{3,35},{35,3},{4,36},{36... | collective-permute-start | bytes 786440 | tf_op jit(solution)/shard_map/ppermute | solution.py:22
  71.6 21.1 %collective-permute-start.15 = (f32[512]{0:T(512)S(1)}, f32[512]{0:T(512)S(1)}, u32[]{:S(2)}, u32[]{:S(2)}) collective-permute-start(f32[512]{0:T(512)S(1)} %broadcast_select_fusion.54), channel_id=1, source_target_pairs={{0,64},{64,0},{1,65},{65,1},{2,66},{66,2},{3,67},{67,3},{4,68},{68... | collective-permute-start | bytes 6152 | tf_op jit(solution)/shard_map/ppermute | solution.py:22
  83.0 16.0 %collective-permute-start.6 = (f32[512,128]{1,0:T(8,128)S(1)}, f32[512,128]{1,0:T(8,128)S(1)}, u32[]{:S(2)}, u32[]{:S(2)}) collective-permute-start(f32[512,128]{1,0:T(8,128)S(1)} %broadcast_select_fusion.27), channel_id=1, source_target_pairs={{0,64},{64,0},{1,65},{65,1},{2,66},{66,2},{3,67},{67,3},{4,68},{68... | collective-permute-start | bytes 786440 | tf_op jit(solution)/shard_map/ppermute | solution.py:22
  92.7 10.1 %collective-permute-start.16 = (f32[512]{0:T(512)S(1)}, f32[512]{0:T(512)S(1)}, u32[]{:S(2)}, u32[]{:S(2)}) collective-permute-start(f32[512]{0:T(512)S(1)} %broadcast_select_fusion.55), channel_id=1, source_target_pairs={{0,128},{128,0},{1,129},{129,1},{2,130},{130,2},{3,131},{131,3},{4... | collective-permute-start | bytes 6152 | tf_op jit(solution)/shard_map/ppermute | solution.py:22
  107.2 9.4 %collective-permute-start.8 = (f32[512,128]{1,0:T(8,128)S(1)}, f32[512,128]{1,0:T(8,128)S(1)}, u32[]{:S(2)}, u32[]{:S(2)}) collective-permute-start(f32[512,128]{1,0:T(8,128)S(1)} %broadcast_select_fusion.29), channel_id=1, source_target_pairs={{0,256},{256,0},{1,257},{257,1},{2,258},{258,2},{3,259},{259,3},{4... | collective-permute-start | bytes 786440 | tf_op jit(solution)/shard_map/ppermute | solution.py:22
  271.6 13.4 %collective-permute-start.19 = (f32[512,128]{1,0:T(8,128)S(1)}, f32[512,128]{1,0:T(8,128)S(1)}, u32[]{:S(2)}, u32[]{:S(2)}) collective-permute-start(f32[512,128]{1,0:T(8,128)S(1)} %broadcast_select_fusion.13), channel_id=1, source_target_pairs={{0,2},{2,0},{1,3},{3,1},{4,6},{6,4},{5,7},{7,5},{8,10},{10,8},{9,1... | collective-permute-start | bytes 786440 | tf_op jit(solution)/shard_map/ppermute | solution.py:22
  285.1 15.8 %collective-permute-start.20 = (f32[512,128]{1,0:T(8,128)S(1)}, f32[512,128]{1,0:T(8,128)S(1)}, u32[]{:S(2)}, u32[]{:S(2)}) collective-permute-start(f32[512,128]{1,0:T(8,128)S(1)} %broadcast_select_fusion.14), channel_id=1, source_target_pairs={{0,4},{4,0},{1,5},{5,1},{2,6},{6,2},{3,7},{7,3},{8,12},{12,8},{9,1... | collective-permute-start | bytes 786440 | tf_op jit(solution)/shard_map/ppermute | solution.py:22
  300.9 19.4 %collective-permute-start.21 = (f32[512,128]{1,0:T(8,128)S(1)}, f32[512,128]{1,0:T(8,128)S(1)}, u32[]{:S(2)}, u32[]{:S(2)}) collective-permute-start(f32[512,128]{1,0:T(8,128)S(1)} %broadcast_select_fusion.15), channel_id=1, source_target_pairs={{0,8},{8,0},{1,9},{9,1},{2,10},{10,2},{3,11},{11,3},{4,12},{12,4},... | collective-permute-start | bytes 786440 | tf_op jit(solution)/shard_map/ppermute | solution.py:22
  320.3 9.3 %collective-permute-start.22 = (f32[512,128]{1,0:T(8,128)S(1)}, f32[512,128]{1,0:T(8,128)S(1)}, u32[]{:S(2)}, u32[]{:S(2)}) collective-permute-start(f32[512,128]{1,0:T(8,128)S(1)} %broadcast_select_fusion.16), channel_id=1, source_target_pairs={{0,16},{16,0},{1,17},{17,1},{2,18},{18,2},{3,19},{19,3},{4,20},{20... | collective-permute-start | bytes 786440 | tf_op jit(solution)/shard_map/ppermute | solution.py:22
  329.6 16.6 %collective-permute-start.23 = (f32[512,128]{1,0:T(8,128)S(1)}, f32[512,128]{1,0:T(8,128)S(1)}, u32[]{:S(2)}, u32[]{:S(2)}) collective-permute-start(f32[512,128]{1,0:T(8,128)S(1)} %broadcast_select_fusion.17), channel_id=1, source_target_pairs={{0,32},{32,0},{1,33},{33,1},{2,34},{34,2},{3,35},{35,3},{4,36},{36... | collective-permute-start | bytes 786440 | tf_op jit(solution)/shard_map/ppermute | solution.py:22
  338.2 12.6 %collective-permute-start.30 = (f32[512]{0:T(512)S(1)}, f32[512]{0:T(512)S(1)}, u32[]{:S(2)}, u32[]{:S(2)}) collective-permute-start(f32[512]{0:T(512)S(1)} %broadcast_select_fusion.42), channel_id=1, source_target_pairs={{0,8},{8,0},{1,9},{9,1},{2,10},{10,2},{3,11},{11,3},{4,12},{12,4},... | collective-permute-start | bytes 6152 | tf_op jit(solution)/shard_map/ppermute | solution.py:22
  346.3 19.1 %collective-permute-start.24 = (f32[512,128]{1,0:T(8,128)S(1)}, f32[512,128]{1,0:T(8,128)S(1)}, u32[]{:S(2)}, u32[]{:S(2)}) collective-permute-start(f32[512,128]{1,0:T(8,128)S(1)} %broadcast_select_fusion.18), channel_id=1, source_target_pairs={{0,64},{64,0},{1,65},{65,1},{2,66},{66,2},{3,67},{67,3},{4,68},{68... | collective-permute-start | bytes 786440 | tf_op jit(solution)/shard_map/ppermute | solution.py:22
  350.8 11.3 %collective-permute-start.31 = (f32[512]{0:T(512)S(1)}, f32[512]{0:T(512)S(1)}, u32[]{:S(2)}, u32[]{:S(2)}) collective-permute-start(f32[512]{0:T(512)S(1)} %broadcast_select_fusion.43), channel_id=1, source_target_pairs={{0,16},{16,0},{1,17},{17,1},{2,18},{18,2},{3,19},{19,3},{4,20},{20... | collective-permute-start | bytes 6152 | tf_op jit(solution)/shard_map/ppermute | solution.py:22
  365.4 13.6 %collective-permute-start.25 = (f32[512,128]{1,0:T(8,128)S(1)}, f32[512,128]{1,0:T(8,128)S(1)}, u32[]{:S(2)}, u32[]{:S(2)}) collective-permute-start(f32[512,128]{1,0:T(8,128)S(1)} %broadcast_select_fusion.19), channel_id=1, source_target_pairs={{0,128},{128,0},{1,129},{129,1},{2,130},{130,2},{3,131},{131,3},{4... | collective-permute-start | bytes 786440 | tf_op jit(solution)/shard_map/ppermute | solution.py:22
  379.0 109.7 %collective-permute-start.26 = (f32[512,128]{1,0:T(8,128)S(1)}, f32[512,128]{1,0:T(8,128)S(1)}, u32[]{:S(2)}, u32[]{:S(2)}) collective-permute-start(f32[512,128]{1,0:T(8,128)S(1)} %broadcast_select_fusion.20), channel_id=1, source_target_pairs={{0,256},{256,0},{1,257},{257,1},{2,258},{258,2},{3,259},{259,3},{4... | collective-permute-start | bytes 786440 | tf_op jit(solution)/shard_map/ppermute | solution.py:22
  383.2 105.5 %collective-permute-start.35 = (f32[512]{0:T(512)S(1)}, f32[512]{0:T(512)S(1)}, u32[]{:S(2)}, u32[]{:S(2)}) collective-permute-start(f32[512]{0:T(512)S(1)} %broadcast_select_fusion.47), channel_id=1, source_target_pairs={{0,256},{256,0},{1,257},{257,1},{2,258},{258,2},{3,259},{259,3},{4... | collective-permute-start | bytes 6152 | tf_op jit(solution)/shard_map/ppermute | solution.py:22
  597.6 9.4 %collective-permute-start.37 = (f32[512,128]{1,0:T(8,128)S(1)}, f32[512,128]{1,0:T(8,128)S(1)}, u32[]{:S(2)}, u32[]{:S(2)}) collective-permute-start(f32[512,128]{1,0:T(8,128)S(1)} %broadcast_select_fusion.4), channel_id=1, source_target_pairs={{0,2},{2,0},{1,3},{3,1},{4,6},{6,4},{5,7},{7,5},{8,10},{10,8},{9,1... | collective-permute-start | bytes 786440 | tf_op jit(solution)/shard_map/ppermute | solution.py:22
  607.1 16.6 %collective-permute-start.38 = (f32[512,128]{1,0:T(8,128)S(1)}, f32[512,128]{1,0:T(8,128)S(1)}, u32[]{:S(2)}, u32[]{:S(2)}) collective-permute-start(f32[512,128]{1,0:T(8,128)S(1)} %broadcast_select_fusion.5), channel_id=1, source_target_pairs={{0,4},{4,0},{1,5},{5,1},{2,6},{6,2},{3,7},{7,3},{8,12},{12,8},{9,1... | collective-permute-start | bytes 786440 | tf_op jit(solution)/shard_map/ppermute | solution.py:22
  623.7 18.9 %collective-permute-start.39 = (f32[512,128]{1,0:T(8,128)S(1)}, f32[512,128]{1,0:T(8,128)S(1)}, u32[]{:S(2)}, u32[]{:S(2)}) collective-permute-start(f32[512,128]{1,0:T(8,128)S(1)} %broadcast_select_fusion.6), channel_id=1, source_target_pairs={{0,8},{8,0},{1,9},{9,1},{2,10},{10,2},{3,11},{11,3},{4,12},{12,4},... | collective-permute-start | bytes 786440 | tf_op jit(solution)/shard_map/ppermute | solution.py:22
  651.1 15.7 %collective-permute-start.41 = (f32[512,128]{1,0:T(8,128)S(1)}, f32[512,128]{1,0:T(8,128)S(1)}, u32[]{:S(2)}, u32[]{:S(2)}) collective-permute-start(f32[512,128]{1,0:T(8,128)S(1)} %broadcast_select_fusion.8), channel_id=1, source_target_pairs={{0,32},{32,0},{1,33},{33,1},{2,34},{34,2},{3,35},{35,3},{4,36},{36... | collective-permute-start | bytes 786440 | tf_op jit(solution)/shard_map/ppermute | solution.py:22
  658.4 12.8 %collective-permute-start.48 = (f32[512]{0:T(512)S(1)}, f32[512]{0:T(512)S(1)}, u32[]{:S(2)}, u32[]{:S(2)}) collective-permute-start(f32[512]{0:T(512)S(1)} %broadcast_select_fusion.33), channel_id=1, source_target_pairs={{0,8},{8,0},{1,9},{9,1},{2,10},{10,2},{3,11},{11,3},{4,12},{12,4},... | collective-permute-start | bytes 6152 | tf_op jit(solution)/shard_map/ppermute | solution.py:22
  666.9 20.4 %collective-permute-start.42 = (f32[512,128]{1,0:T(8,128)S(1)}, f32[512,128]{1,0:T(8,128)S(1)}, u32[]{:S(2)}, u32[]{:S(2)}) collective-permute-start(f32[512,128]{1,0:T(8,128)S(1)} %broadcast_select_fusion.9), channel_id=1, source_target_pairs={{0,64},{64,0},{1,65},{65,1},{2,66},{66,2},{3,67},{67,3},{4,68},{68... | collective-permute-start | bytes 786440 | tf_op jit(solution)/shard_map/ppermute | solution.py:22
  671.3 11.1 %collective-permute-start.49 = (f32[512]{0:T(512)S(1)}, f32[512]{0:T(512)S(1)}, u32[]{:S(2)}, u32[]{:S(2)}) collective-permute-start(f32[512]{0:T(512)S(1)} %broadcast_select_fusion.34), channel_id=1, source_target_pairs={{0,16},{16,0},{1,17},{17,1},{2,18},{18,2},{3,19},{19,3},{4,20},{20... | collective-permute-start | bytes 6152 | tf_op jit(solution)/shard_map/ppermute | solution.py:22
  687.3 13.6 %collective-permute-start.43 = (f32[512,128]{1,0:T(8,128)S(1)}, f32[512,128]{1,0:T(8,128)S(1)}, u32[]{:S(2)}, u32[]{:S(2)}) collective-permute-start(f32[512,128]{1,0:T(8,128)S(1)} %broadcast_select_fusion.10), channel_id=1, source_target_pairs={{0,128},{128,0},{1,129},{129,1},{2,130},{130,2},{3,131},{131,3},{4... | collective-permute-start | bytes 786440 | tf_op jit(solution)/shard_map/ppermute | solution.py:22
  700.9 107.0 %collective-permute-start.44 = (f32[512,128]{1,0:T(8,128)S(1)}, f32[512,128]{1,0:T(8,128)S(1)}, u32[]{:S(2)}, u32[]{:S(2)}) collective-permute-start(f32[512,128]{1,0:T(8,128)S(1)} %broadcast_select_fusion.11), channel_id=1, source_target_pairs={{0,256},{256,0},{1,257},{257,1},{2,258},{258,2},{3,259},{259,3},{4... | collective-permute-start | bytes 786440 | tf_op jit(solution)/shard_map/ppermute | solution.py:22
  703.4 103.9 %collective-permute-start.53 = (f32[512]{0:T(512)S(1)}, f32[512]{0:T(512)S(1)}, u32[]{:S(2)}, u32[]{:S(2)}) collective-permute-start(f32[512]{0:T(512)S(1)} %broadcast_select_fusion.38), channel_id=1, source_target_pairs={{0,256},{256,0},{1,257},{257,1},{2,258},{258,2},{3,259},{259,3},{4... | collective-permute-start | bytes 6152 | tf_op jit(solution)/shard_map/ppermute | solution.py:22
  (32 other events, 576.1 us)
where the time goes:
time: 815 us; the launch traced here: 810 us
  blocking collectives  198 us (24%)
  starting transfers between devices  194 us (24%)
  waiting for transfers between devices  141 us (17%)
  loops' own time  106 us (13%)
  other arithmetic  55.7 us (7%)
  matrix products  50.8 us (6%)
  local copies, waits for them, and re-layouts  44.5 us (5%)
  between operations  19.2 us (2%)
    psum x2, blocking collectives, on_device(): total_err, total_obs = lax.psum((err_sum, obs_sum), 'blk')  198 us
    ppermute x54, starting transfers between devices, from_partner(): return lax.ppermute(block, axis, route)  194 us
    ppermute x54, waiting for transfers between devices, from_partner(): return lax.ppermute(block, axis, route)  141 us
    another operation x2, loops' own time, on_device(): result = lax.fori_loop(0, rows.shape[0], advance, init)  106 us
    dot_general x32, matrix products, tile_step(): lax.dot_general(uh, vh, (((1,), (1,)), ((), ())), preferred_element_type=...  40 us
    reduce_sum x32, other arithmetic, tile_step(): obs_sum = obs_sum + jnp.where(active, jnp.sum(obs), jnp.float32(0.0))  33.4 us
    dynamic_slice x32, local copies, waits for them, and re-layouts, tile_step(): row0 = rows[t] * edge  18.8 us
    dynamic_slice x32, local copies, waits for them, and re-layouts, tile_step(): col0 = cols[t] * edge  18.6 us
  transfers between devices with their start and end apart: 54, of which 28 were waited for; matrix products, arithmetic and copies ran while one was open for 1% of the time, Pallas kernels for 0%

commit v1 on v0

v1 whole, which is shorter than its diff:
```python
import functools

import jax
import jax.numpy as jnp
from jax import lax
from jax.experimental import pallas as pl
from jax.experimental.pallas import tpu as pltpu
from jax.sharding import PartitionSpec as P

SUBEP = 2
TILE = 128
ROW_TILES = 8
COL_TILES = 4
ITEM_ROWS = COL_TILES * TILE
PACKED = ITEM_ROWS + 8

step_scale = 0.8
bias_rate = 0.005
shrink = 0.02
mean_rate = 0.5

F32 = jnp.float32
BF16 = jnp.bfloat16
MESH = pl.DeviceIdType.MESH

STAGE_A = (1, 2, 3, 7)
STAGE_B = (4, 5, 6, 8)
CORE_BIT = 0
SUM_A = ((1, 2), (2, 8))
SUM_B = ((16, 8), (128, 4))


def flipped(me, bits):
    other = me
    for bit in bits:
        taken = lax.rem(lax.div(me, 1 << bit), 2)
        other = other + (1 - 2 * taken) * (1 << bit)
    return other


def group_peer(me, stride, size, ahead):
    place = lax.rem(lax.div(me, stride), size)
    return me + (lax.rem(place + ahead, size) - place) * stride


def stage_kernel(bits, rounds, x_ref, s_ref, y_ref, t_ref, *scratch):
    held, got = scratch[0], scratch[1 : 1 + len(rounds)]
    x_send, x_recv, s_send, s_recv = scratch[1 + len(rounds) :]
    me = lax.axis_index("blk")
    partner = flipped(me, bits)
    peers = [[group_peer(me, stride, size, k) for k in range(1, size)] for stride, size in rounds]
    greeted = ([partner] if bits else []) + [peer for group in peers for peer in group]

    barrier = pltpu.get_barrier_semaphore()
    for device in greeted:
        pl.semaphore_signal(barrier, inc=1, device_id=(device,), device_id_type=MESH)
    pl.semaphore_wait(barrier, len(greeted))

    if bits:
        block = pltpu.make_async_remote_copy(
            src_ref=x_ref, dst_ref=y_ref, send_sem=x_send, recv_sem=x_recv,
            device_id=(partner,), device_id_type=MESH,
        )
    else:
        block = pltpu.make_async_copy(x_ref, y_ref, x_recv)
    block.start()

    if rounds:
        total = s_ref[...]
        for r, group in enumerate(peers):
            held[r] = total
            for k, peer in enumerate(group):
                pltpu.make_async_remote_copy(
                    src_ref=held.at[r], dst_ref=got[r].at[k], send_sem=s_send.at[r], recv_sem=s_recv.at[r],
                    device_id=(peer,), device_id_type=MESH,
                ).start()
            pltpu.make_async_copy(got[r], got[r], s_recv.at[r]).wait()
            total = total + jnp.sum(got[r][...], axis=0)
        t_ref[...] = total
        for r in range(len(rounds)):
            pltpu.make_async_copy(got[r], got[r], s_send.at[r]).wait()
    else:
        t_ref[...] = s_ref[...]
    block.wait()


def stage_call(bits, rounds, collective_id, x, s):
    anywhere = pl.BlockSpec(memory_space=pl.ANY)
    vmem = pl.BlockSpec(memory_space=pltpu.VMEM)
    return pl.pallas_call(
        functools.partial(stage_kernel, bits, rounds),
        out_shape=(jax.ShapeDtypeStruct(x.shape, x.dtype), jax.ShapeDtypeStruct(s.shape, s.dtype)),
        in_specs=[anywhere, vmem],
        out_specs=(anywhere, vmem),
        scratch_shapes=[
            pltpu.VMEM((max(1, len(rounds)),) + s.shape, F32),
            *[pltpu.VMEM((size - 1,) + s.shape, F32) for _, size in rounds],
            pltpu.SemaphoreType.DMA,
            pltpu.SemaphoreType.DMA,
            pltpu.SemaphoreType.DMA((max(1, len(rounds)),)),
            pltpu.SemaphoreType.DMA((max(1, len(rounds)),)),
        ],
        compiler_params=pltpu.CompilerParams(collective_id=collective_id, has_side_effects=True),
        name=f"exchange_{collective_id}",
    )(x, s)


def stage(mask, stage_bits, rounds, first_id, x, s):
    choice = sum(jnp.bitwise_and(jnp.right_shift(mask, bit), 1) << k for k, bit in enumerate(stage_bits))

    def branch(value):
        bits = tuple(bit for k, bit in enumerate(stage_bits) if value >> k & 1)
        return lambda x, s: stage_call(bits, rounds, first_id + value, x, s)

    return lax.switch(choice, [branch(value) for value in range(1 << len(stage_bits))], x, s)


def exchange(mask, x, s):
    x, s = stage(mask, STAGE_A, SUM_A, 0, x, s)
    x, s = stage(mask, STAGE_B, SUM_B, 16, x, s)
    flip = jnp.bitwise_and(jnp.right_shift(mask, CORE_BIT), 1)

    def cross(x, s):
        return stage_call((CORE_BIT,), (), 32, x, s)

    return lax.cond(flip == 1, cross, lambda x, s: (x, s), x, s)


def sub_epoch_kernel(
    sub, rows, cols, counts, mean_in, totals, users_in, ubias_in, packed_in, ratings, observed,
    users, ubias, packed, sums, mean_out,
    ubias_wide, items_t, ibias_wide, rating_buf, seen_buf, rating_sem, seen_sem,
):
    count = counts[sub]

    def fetch(t):
        return (
            pltpu.make_async_copy(ratings.at[sub, 0, t], rating_buf.at[t], rating_sem.at[t]),
            pltpu.make_async_copy(observed.at[sub, 0, t], seen_buf.at[t], seen_sem.at[t]),
        )

    def start(t, carry):
        for copy in fetch(t):
            copy.start()
        return carry

    lax.fori_loop(0, count, start, 0)

    mean = mean_in[...]
    if sub:
        total = jnp.sum(totals[...], axis=1, keepdims=True)
        mean = mean + mean_rate * total[0:1] / total[1:2]
    mean_out[...] = jnp.broadcast_to(mean, (1, TILE))
    mean = jnp.broadcast_to(mean, (8, TILE))

    diagonal = lax.broadcasted_iota(jnp.int32, (TILE, TILE), 0) == lax.broadcasted_iota(jnp.int32, (TILE, TILE), 1)
    for a in range(ROW_TILES):
        across = jnp.where(diagonal, ubias_in[a : a + 1, :], 0.0)
        ubias_wide[a * TILE : (a + 1) * TILE, :] = jnp.broadcast_to(
            jnp.sum(across, axis=1, keepdims=True), (TILE, TILE)
        )
        users[a * TILE : (a + 1) * TILE, :] = users_in[a * TILE : (a + 1) * TILE, :]
    for c in range(COL_TILES):
        items_t[c] = packed_in[c * TILE : (c + 1) * TILE, :].T
        ibias_wide[c] = jnp.broadcast_to(packed_in[ITEM_ROWS + c : ITEM_ROWS + c + 1, :], (8, TILE))

    learn_rate = step_scale / TILE

    def slot(t, carry):
        err_sum, obs_sum = carry
        row0 = pl.multiple_of(rows[sub, t] * TILE, TILE)
        c = cols[sub, t]
        for copy in fetch(t):
            copy.wait()
        u = users[pl.ds(row0, TILE), :]
        bu = ubias_wide[pl.ds(row0, TILE), :]
        vt = items_t[c]
        bv = ibias_wide[c]
        uh = u.astype(BF16)
        vht = vt.astype(BF16)
        obs = seen_buf[t].astype(F32)
        known = rating_buf[t].astype(F32) - bu
        known = (known.reshape(TILE // 8, 8, TILE) - (mean + bv)[None]).reshape(TILE, TILE)
        score = jnp.dot(uh, vht, preferred_element_type=F32)
        err = obs * (known - score)
        eh = err.astype(BF16)
        grad_u = lax.dot_general(eh, vht, (((1,), (1,)), ((), ())), preferred_element_type=F32)
        grad_vt = jnp.dot(uh.T, eh, preferred_element_type=F32)
        err_rows = jnp.sum(err, axis=1, keepdims=True)
        err_cols = jnp.sum(err.reshape(TILE // 8, 8, TILE), axis=0)
        users[pl.ds(row0, TILE), :] = u + learn_rate * (grad_u - shrink * u)
        items_t[c] = vt + learn_rate * (grad_vt - shrink * vt)
        ubias_wide[pl.ds(row0, TILE), :] = bu + bias_rate * (err_rows - shrink * bu)
        ibias_wide[c] = bv + bias_rate * (jnp.sum(err_cols, axis=0, keepdims=True) - shrink * bv)
        return err_sum + err_cols, obs_sum + jnp.sum(obs.reshape(TILE // 8, 8, TILE), axis=0)

    zero = jnp.zeros((8, TILE), F32)
    err_sum, obs_sum = lax.fori_loop(0, count, slot, (zero, zero))

    sums[0:1, :] = jnp.sum(err_sum, axis=0, keepdims=True)
    sums[1:2, :] = jnp.sum(obs_sum, axis=0, keepdims=True)
    sums[2:8, :] = jnp.zeros((6, TILE), F32)
    for a in range(ROW_TILES):
        wide = ubias_wide[a * TILE : (a + 1) * TILE, :]
        ubias[a : a + 1, :] = jnp.sum(jnp.where(diagonal, wide, 0.0), axis=0, keepdims=True)
    for c in range(COL_TILES):
        packed[c * TILE : (c + 1) * TILE, :] = items_t[c].T
        packed[ITEM_ROWS + c : ITEM_ROWS + c + 1, :] = ibias_wide[c][0:1, :]
    packed[ITEM_ROWS + COL_TILES : PACKED, :] = jnp.zeros((PACKED - ITEM_ROWS - COL_TILES, TILE), F32)


def sub_epoch(sub, rows, cols, counts, mean, totals, users, ubias, packed, ratings, observed):
    smem = pl.BlockSpec(memory_space=pltpu.SMEM)
    vmem = pl.BlockSpec(memory_space=pltpu.VMEM)
    anywhere = pl.BlockSpec(memory_space=pl.ANY)
    slots = ratings.shape[2]
    shape = lambda *dims: jax.ShapeDtypeStruct(dims, F32)
    return pl.pallas_call(
        functools.partial(sub_epoch_kernel, sub),
        out_shape=(shape(*users.shape), shape(*ubias.shape), shape(*packed.shape), shape(8, TILE), shape(1, TILE)),
        in_specs=[smem, smem, smem, vmem, vmem, vmem, vmem, vmem, anywhere, anywhere],
        out_specs=(vmem,) * 5,
        scratch_shapes=[
            pltpu.VMEM((ROW_TILES * TILE, TILE), F32),
            pltpu.VMEM((COL_TILES, TILE, TILE), F32),
            pltpu.VMEM((COL_TILES, 8, TILE), F32),
            pltpu.VMEM((slots, TILE, TILE), BF16),
            pltpu.VMEM((slots, TILE, TILE), jnp.int32),
            pltpu.SemaphoreType.DMA((slots,)),
            pltpu.SemaphoreType.DMA((slots,)),
        ],
        compiler_params=pltpu.CompilerParams(vmem_limit_bytes=24 << 20),
        name=f"sub_epoch_{sub}",
    )(rows, cols, counts, mean, totals, users, ubias, packed, ratings, observed)


def on_device(
    users,
    user_bias,
    items,
    item_bias,
    global_mean,
    item_owner,
    tile_rows,
    tile_cols,
    tile_counts,
    ratings,
    observed,
):
    masks = jnp.bitwise_xor(item_owner[:, 0], lax.axis_index("blk"))
    rows, cols, counts = tile_rows[:, 0], tile_cols[:, 0], tile_counts[:, 0]
    ubias = user_bias.reshape(ROW_TILES, TILE)
    pad = jnp.zeros((PACKED - ITEM_ROWS - COL_TILES, TILE), F32)
    packed = jnp.concatenate([items, item_bias.reshape(COL_TILES, TILE), pad], axis=0)
    mean = global_mean.reshape(1, 1)
    sums = jnp.zeros((8, TILE), F32)

    packed, totals = exchange(masks[0], packed, sums)
    users, ubias, packed, sums, mean = sub_epoch(
        0, rows, cols, counts, mean, totals, users, ubias, packed, ratings, observed
    )
    packed, totals = exchange(jnp.bitwise_xor(masks[0], masks[1]), packed, sums)
    users, ubias, packed, sums, mean = sub_epoch(
        1, rows, cols, counts, mean[:, :1], totals, users, ubias, packed, ratings, observed
    )
    packed, totals = exchange(masks[1], packed, sums)
    total = jnp.sum(totals, axis=1)
    mean = mean[0, 0] + mean_rate * total[0] / total[1]
    return (
        users,
        ubias.reshape(-1),
        packed[:ITEM_ROWS],
        packed[ITEM_ROWS : ITEM_ROWS + COL_TILES].reshape(-1),
        mean,
    )


def solution(mesh):
    in_specs = (
        P("blk", None),
        P("blk"),
        P("blk", None),
        P("blk"),
        P(),
        P(None, "blk"),
        P(None, "blk", None),
        P(None, "blk", None),
        P(None, "blk"),
        P(None, "blk", None, None, None),
        P(None, "blk", None, None, None),
    )
    out_specs = (P("blk", None), P("blk"), P("blk", None), P("blk"), P())
    return jax.shard_map(
        on_device, mesh=mesh, in_specs=in_specs, out_specs=out_specs, check_vma=False
    )
```

time: 815 us -> 179 us (0.22)
  blocking collectives: 198 us -> 0 us
  starting transfers between devices: 194 us -> 0 us
  Pallas kernels: 0 us -> 148 us
  waiting for transfers between devices: 141 us -> 0 us
  loops' own time: 106 us -> 0.56 us
  other arithmetic: 55.7 us -> 1.87 us
  matrix products: 50.8 us -> 0 us
  local copies, waits for them, and re-layouts: 44.5 us -> 10.6 us
    psum x2 -> x0, blocking collectives: 198 us -> none  [on_device(): total_err, total_obs = lax.psum((err_sum, obs_sum), 'blk')]
    ppermute x54 -> x0, starting transfers between devices: 194 us -> none  [from_partner(): return lax.ppermute(block, axis, route)]
    pallas_call x0 -> x10, Pallas kernels: none -> 148 us  [the longest x8 132 us: stage_call(): pl.pallas_call(functools.partial(stage_kernel, bits, rounds), out_shape=(...]
    ppermute x54 -> x0, waiting for transfers between devices: 141 us -> none  [from_partner(): return lax.ppermute(block, axis, route)]
    another operation x2 -> x9, loops' own time: 106 us -> 0.56 us  [the longest x6 0.52 us: stage(): lax.switch(choice, [branch(value) for value in range(1 << len(stage_bits)...]
    dot_general x96 -> x0, matrix products: 50.8 us -> none  [the longest x32 40 us: tile_step(): lax.dot_general(uh, vh, (((1,), (1,)), ((), ())), preferred_element_type=...]
    dynamic_slice x96 -> x0, local copies, waits for them, and re-layouts: 39.9 us -> none  [the longest x32 18.8 us: tile_step(): row0 = rows[t] * edge]
    reduce_sum x32 -> x1, other arithmetic: 33.4 us -> 0.12 us  [on_device(): total = jnp.sum(totals, axis=1)]
  transfers between devices with their start and end apart: 54 -> 0, of which waited for: 28 -> 0; matrix products, arithmetic and copies ran while one was open for 1% -> 0% of each run, Pallas kernels for 0% -> 0%
where the time goes in v1:
time: 179 us; the launch traced here: 178 us
  Pallas kernels  148 us (83%)
  between operations  17 us (9%)
  local copies, waits for them, and re-layouts  10.6 us (6%)
  other arithmetic  1.87 us (1%)
    pallas_call x8, Pallas kernels, stage_call(): pl.pallas_call(functools.partial(stage_kernel, bits, rounds), out_shape=(...  132 us
    pallas_call x2, Pallas kernels, sub_epoch(): pl.pallas_call(functools.partial(sub_epoch_kernel, sub), out_shape=(shape...  16.5 us
    cond x4, local copies, waits for them, and re-layouts  4.53 us

profile of v1, /device:TPU:1, one launch (start us, length us, event | category | flops | bytes accessed | tf_op | source)
XLA Modules:
  0.0 178.1 jit_solution(713431428171765471)
XLA Ops:
  0.6 0.7 broadcast_xor_fusion
  1.3 0.6 fusion.1
  4.6 1.1 maximum_maximum_fusion
  5.7 16.7 %conditional.9 = ((f32[520,128]{1,0:T(8,128)S(1)}, f32[8,128]{1,0:T(8,128)S(1)})) conditional(s32[]{:T(128)} %bitcast.6, f32[520,128]{1,0:T(8,128)S(1)} %maximum_maximum_fusion, f32[520,128]{1,0:T(8,128)S(1)} %maximum_maximum_fusion, f32[520,128]{1,0:T(8,128)S(1)} %maximum_maximum_fusion, ...), branch_computations={%region_0.0_spmd, %region_1.0_spmd, %region_2.0_spmd, %region_3.0_... | conditional | bytes 4108 | solution.py:115
  5.7 0.6 broadcast_in_dim.43.s_ref
  6.3 16.0 %exchange_9.3 = (f32[520,128]{1,0:T(8,128)S(1)}, f32[8,128]{1,0:T(8,128)S(1)}) custom-call(f32[520,128]{1,0:T(8,128)S(1)} %x_ref.9, f32[8,128]{1,0:T(8,128)} %broadcast_in_dim.43.s_ref), custom_call_target="tpu_custom_call" | custom-call | tf_op jit(solution)/shard_map/cond/branch_9_fun/exchange_9/pallas_call | solution.py:90
  25.0 28.0 %conditional.10 = ((f32[520,128]{1,0:T(8,128)}, f32[8,128]{1,0:T(8,128)S(1)})) conditional(s32[]{:T(128)} %bitcast.5, (f32[520,128]{1,0:T(8,128)S(1)}, f32[8,128]{1,0:T(8,128)S(1)}) %get-tuple-element.822, (f32[520,128]{1,0:T(8,128)S(1)}, f32[8,128]{1,0:T(8,128)S(1)}) %get-tuple-element.822, ...), branch_computations={%region_16.0_spmd, %region_17.0_spmd, %region_18.0_spmd, %region_1... | conditional | bytes 8 | solution.py:115
  25.1 28.0 %exchange_26.3 = (f32[520,128]{1,0:T(8,128)}, f32[8,128]{1,0:T(8,128)S(1)}) custom-call(f32[520,128]{1,0:T(8,128)S(1)} %get-tuple-element.407.x_ref, f32[8,128]{1,0:T(8,128)S(1)} %get-tuple-element.408.s_ref), custom_call_target="tpu_custom_call" | custom-call | tf_op jit(solution)/shard_map/cond/branch_10_fun/exchange_26/pallas_call | solution.py:90
  53.7 6.6 %conditional.11 = ((f32[520,128]{1,0:T(8,128)}, f32[8,128]{1,0:T(8,128)S(1)})) conditional(s32[]{:T(128)} %bitcast.4, (f32[520,128]{1,0:T(8,128)}, f32[8,128]{1,0:T(8,128)S(1)}) %get-tuple-element.823, (f32[520,128]{1,0:T(8,128)}, f32[8,128]{1,0:T(8,128)S(1)}) %get-tuple-element.823), branch_computations={%region_32.0_spmd, %region_33.0_spmd} | conditional | bytes 540680 | solution.py:126
  53.7 1.7 copy.227.x_ref
  55.4 0.6 copy.228.s_ref
  56.0 4.3 %exchange_32.5 = (f32[520,128]{1,0:T(8,128)}, f32[8,128]{1,0:T(8,128)S(1)}) custom-call(f32[520,128]{1,0:T(8,128)} %copy.227.x_ref, f32[8,128]{1,0:T(8,128)} %copy.228.s_ref), custom_call_target="tpu_custom_call" | custom-call | tf_op jit(solution)/shard_map/cond/branch_1_fun/exchange_32/pallas_call | solution.py:90
  61.0 1.0 copy-done.2
  62.0 8.5 %sub_epoch_0.1 = (f32[1024,128]{1,0:T(8,128)S(1)}, f32[8,128]{1,0:T(8,128)S(1)}, f32[520,128]{1,0:T(8,128)S(1)}, f32[8,128]{1,0:T(8,128)S(1)}, f32[1,128]{1,0:T(1,128)S(1)}) custom-call(s32[2,16]{1,0:T(2,128)S(1)} %bitcast.24, s32[2,16]{1,0:T(2,128)S(1)} %bitcast.26, s32[2]{0:T(128)S(1)} %bitcast.28, f32[1,1]{1,0:T(1,128)} %bitcast.22.mean_in, ...), custom_call_target="tpu_custom_call" | custom-call | tf_op jit(solution)/shard_map/sub_epoch_0/pallas_call | solution.py:218
  70.5 0.8 copy-done.3
  72.6 17.2 %conditional.12 = ((f32[520,128]{1,0:T(8,128)}, f32[8,128]{1,0:T(8,128)S(1)})) conditional(s32[]{:T(128)} %bitcast.11, (f32[520,128]{1,0:T(8,128)S(1)}, f32[8,128]{1,0:T(8,128)S(1)}) %tuple.275, (f32[520,128]{1,0:T(8,128)S(1)}, f32[8,128]{1,0:T(8,128)S(1)}) %tuple.275, (f32[520,128]{1,0:T(8,128)S(1)}, ...), branch_computations={%region_34.0_spmd, %region_35.0_spmd, %region_36.0_spmd, %region_3... | conditional | bytes 8 | solution.py:115
  72.7 17.2 %exchange_14.4 = (f32[520,128]{1,0:T(8,128)}, f32[8,128]{1,0:T(8,128)S(1)}) custom-call(f32[520,128]{1,0:T(8,128)S(1)} %get-tuple-element.449.x_ref, f32[8,128]{1,0:T(8,128)S(1)} %get-tuple-element.450.s_ref), custom_call_target="tpu_custom_call" | custom-call | tf_op jit(solution)/shard_map/cond/branch_14_fun/exchange_14/pallas_call | solution.py:90
  89.8 20.8 %conditional.13 = ((f32[520,128]{1,0:T(8,128)}, f32[8,128]{1,0:T(8,128)S(1)})) conditional(s32[]{:T(128)} %bitcast.10, (f32[520,128]{1,0:T(8,128)}, f32[8,128]{1,0:T(8,128)S(1)}) %get-tuple-element.825, (f32[520,128]{1,0:T(8,128)}, f32[8,128]{1,0:T(8,128)S(1)}) %get-tuple-element.825, (f32[520,128]{1,0:T(8,128)}, ...), branch_computations={%region_50.0_spmd, %region_51.0_spmd, %region_52.0_spmd, %region_5... | conditional | bytes 8 | solution.py:115
  89.9 20.5 %exchange_31.4 = (f32[520,128]{1,0:T(8,128)}, f32[8,128]{1,0:T(8,128)S(1)}) custom-call(f32[520,128]{1,0:T(8,128)} %get-tuple-element.483.x_ref, f32[8,128]{1,0:T(8,128)S(1)} %get-tuple-element.484.s_ref), custom_call_target="tpu_custom_call" | custom-call | tf_op jit(solution)/shard_map/cond/branch_15_fun/exchange_31/pallas_call | solution.py:90
  110.6 7.3 %conditional.14 = ((f32[520,128]{1,0:T(8,128)}, f32[8,128]{1,0:T(8,128)S(1)})) conditional(s32[]{:T(128)} %bitcast.9, (f32[520,128]{1,0:T(8,128)}, f32[8,128]{1,0:T(8,128)S(1)}) %get-tuple-element.826, (f32[520,128]{1,0:T(8,128)}, f32[8,128]{1,0:T(8,128)S(1)}) %get-tuple-element.826), branch_computations={%region_66.0_spmd, %region_67.0_spmd} | conditional | bytes 540680 | solution.py:126
  110.6 1.7 copy.229.x_ref
  112.3 0.6 copy.230.s_ref
  112.9 5.0 %exchange_32.6 = (f32[520,128]{1,0:T(8,128)}, f32[8,128]{1,0:T(8,128)S(1)}) custom-call(f32[520,128]{1,0:T(8,128)} %copy.229.x_ref, f32[8,128]{1,0:T(8,128)} %copy.230.s_ref), custom_call_target="tpu_custom_call" | custom-call | tf_op jit(solution)/shard_map/cond/branch_1_fun/exchange_32/pallas_call | solution.py:90
  117.9 1.0 copy-done.4
  118.9 8.0 %sub_epoch_1.1 = (f32[1024,128]{1,0:T(8,128)}, f32[8,128]{1,0:T(8,128)}, f32[520,128]{1,0:T(8,128)S(1)}, f32[8,128]{1,0:T(8,128)S(1)}, f32[1,128]{1,0:T(1,128)S(1)}) custom-call(s32[2,16]{1,0:T(2,128)S(1)} %bitcast.25, s32[2,16]{1,0:T(2,128)S(1)} %bitcast.27, s32[2]{0:T(128)S(1)} %bitcast.29, f32[1,1]{1,0:T(1,128)S(1)} %bitcast.30, ...), custom_call_target="tpu_custom_call" | custom-call | tf_op jit(solution)/shard_map/sub_epoch_1/pallas_call | solution.py:218
  129.6 18.6 %conditional.15 = ((f32[520,128]{1,0:T(8,128)S(1)}, f32[8,128]{1,0:T(8,128)S(1)})) conditional(s32[]{:T(128)} %bitcast.15, (f32[520,128]{1,0:T(8,128)S(1)}, f32[8,128]{1,0:T(8,128)S(1)}) %tuple.276, (f32[520,128]{1,0:T(8,128)S(1)}, f32[8,128]{1,0:T(8,128)S(1)}) %tuple.276, (f32[520,128]{1,0:T(8,128)S(1)}, ...), branch_computations={%region_68.0_spmd, %region_69.0_spmd, %region_70.0_spmd, %region_7... | conditional | bytes 8 | solution.py:115
  129.6 18.5 %exchange_7.5 = (f32[520,128]{1,0:T(8,128)S(1)}, f32[8,128]{1,0:T(8,128)S(1)}) custom-call(f32[520,128]{1,0:T(8,128)S(1)} %get-tuple-element.501.x_ref, f32[8,128]{1,0:T(8,128)S(1)} %get-tuple-element.502.s_ref), custom_call_target="tpu_custom_call" | custom-call | tf_op jit(solution)/shard_map/cond/branch_7_fun/exchange_7/pallas_call | solution.py:90
  150.7 22.1 %conditional.16 = ((f32[520,128]{1,0:T(8,128)S(1)}, f32[8,128]{1,0:T(8,128)S(1)})) conditional(s32[]{:T(128)} %bitcast.14, (f32[520,128]{1,0:T(8,128)S(1)}, f32[8,128]{1,0:T(8,128)S(1)}) %get-tuple-element.828, (f32[520,128]{1,0:T(8,128)S(1)}, f32[8,128]{1,0:T(8,128)S(1)}) %get-tuple-element.828, ...), branch_computations={%region_84.0_spmd, %region_85.0_spmd, %region_86.0_spmd, %region_8... | conditional | bytes 8 | solution.py:115
  150.8 22.1 %exchange_21.5 = (f32[520,128]{1,0:T(8,128)S(1)}, f32[8,128]{1,0:T(8,128)S(1)}) custom-call(f32[520,128]{1,0:T(8,128)S(1)} %get-tuple-element.529.x_ref, f32[8,128]{1,0:T(8,128)S(1)} %get-tuple-element.530.s_ref), custom_call_target="tpu_custom_call" | custom-call | tf_op jit(solution)/shard_map/cond/branch_5_fun/exchange_21/pallas_call | solution.py:90
  173.7 0.6 fusion
  175.6 0.7 slice.55
  176.4 0.6 slice_bitcast_fusion
  (19 shorter events, 0.3 us)
Async XLA Ops:
  25.0 36.0 %copy-start = (s32[2,1,16,128,128]{4,3,2,1,0:T(8,128)S(1)}, s32[2,1,16,128,128]{4,3,2,1,0:T(8,128)}, u32[]{:S(2)}) copy-start(s32[2,1,16,128,128]{4,3,2,1,0:T(8,128)} %observed.3) | copy-start | bytes 6291460
  25.0 36.0 %copy-start.1 = (bf16[2,1,16,128,128]{4,3,2,1,0:T(8,128)(2,1)S(1)}, bf16[2,1,16,128,128]{4,3,2,1,0:T(8,128)(2,1)}, u32[]{:S(2)}) copy-start(bf16[2,1,16,128,128]{4,3,2,1,0:T(8,128)(2,1)} %ratings.3) | copy-start | bytes 3145732
  25.0 35.9 %copy-start.5 = (f32[1024]{0:T(1024)S(1)}, f32[1024]{0:T(1024)}, u32[]{:S(2)}) copy-start(f32[1024]{0:T(1024)} %param.114) | copy-start | bytes 12292
  25.0 35.9 %copy-start.6 = (s32[2,1,16]{2,1,0:T(1,128)S(1)}, s32[2,1,16]{2,1,0:T(1,128)}, u32[]{:S(2)}) copy-start(s32[2,1,16]{2,1,0:T(1,128)} %param.119) | copy-start | bytes 388
  25.0 35.9 %copy-start.7 = (s32[2,1,16]{2,1,0:T(1,128)S(1)}, s32[2,1,16]{2,1,0:T(1,128)}, u32[]{:S(2)}) copy-start(s32[2,1,16]{2,1,0:T(1,128)} %param.120) | copy-start | bytes 388
  25.0 35.9 %copy-start.8 = (s32[2,1]{0,1:T(1,128)S(1)}, s32[2,1]{0,1:T(1,128)}, u32[]{:S(2)}) copy-start(s32[2,1]{0,1:T(1,128)} %param.121) | copy-start | bytes 28
  61.0 1.0 copy-start.2
  70.5 0.8 copy-start.3
  117.9 1.0 copy-start.4

commit v2 on v1

--- a/solution.py
+++ b/solution.py
@@ -25,9 +25,9 @@
 
 STAGE_A = (1, 2, 3, 7)
 STAGE_B = (4, 5, 6, 8)
-CORE_BIT = 0
-SUM_A = ((1, 2), (2, 8))
-SUM_B = ((16, 8), (128, 4))
+SUM_A = ((1, 2), (16, 8))
+SUM_B = ((2, 8), (128, 4))
+PIECES = ((0, 264), (264, 256))
 
 
 def flipped(me, bits):
@@ -43,93 +43,122 @@
     return me + (lax.rem(place + ahead, size) - place) * stride
 
 
-def stage_kernel(bits, rounds, x_ref, s_ref, y_ref, t_ref, *scratch):
+def stage_kernel(bits, rounds, hand_on, x_ref, s_ref, y_ref, t_ref, *scratch):
     held, got = scratch[0], scratch[1 : 1 + len(rounds)]
-    x_send, x_recv, s_send, s_recv = scratch[1 + len(rounds) :]
+    x_send, x_recv, s_send, s_recv, h_send, h_recv = scratch[1 + len(rounds) :]
     me = lax.axis_index("blk")
     partner = flipped(me, bits)
+    sibling = flipped(me, (0,))
     peers = [[group_peer(me, stride, size, k) for k in range(1, size)] for stride, size in rounds]
-    greeted = ([partner] if bits else []) + [peer for group in peers for peer in group]
+    greeted = [peer for group in peers for peer in group]
+    if bits:
+        greeted = greeted + [partner]
+    if hand_on:
+        greeted = greeted + [sibling]
 
     barrier = pltpu.get_barrier_semaphore()
     for device in greeted:
         pl.semaphore_signal(barrier, inc=1, device_id=(device,), device_id_type=MESH)
     pl.semaphore_wait(barrier, len(greeted))
 
+    def part(ref, piece):
+        return ref.at[pl.ds(piece[0], piece[1])]
+
+    here = y_ref.at[0] if hand_on else y_ref
+    blocks = []
+    for k, piece in enumerate(PIECES):
+        if bits:
+            block = pltpu.make_async_remote_copy(
+                src_ref=part(x_ref, piece), dst_ref=part(here, piece), send_sem=x_send.at[k], recv_sem=x_recv.at[k],
+                device_id=(partner,), device_id_type=MESH,
+            )
+        else:
+            block = pltpu.make_async_copy(part(x_ref, piece), part(here, piece), x_recv.at[k])
+        blocks.append(block)
+
+    total = s_ref[...]
+    for r, group in enumerate(peers):
+        held[r] = total
+        for k, peer in enumerate(group):
+            pltpu.make_async_remote_copy(
+                src_ref=held.at[r], dst_ref=got[r].at[k], send_sem=s_send.at[r], recv_sem=s_recv.at[r],
+                device_id=(peer,), device_id_type=MESH,
+            ).start()
+        if r == 0:
+            for block in blocks:
+                block.start()
+        pltpu.make_async_copy(got[r], got[r], s_recv.at[r]).wait()
+        total = total + jnp.sum(got[r][...], axis=0)
+    t_ref[...] = total
+    for r in range(len(rounds)):
+        pltpu.make_async_copy(got[r], got[r], s_send.at[r]).wait()
+
+    handed = []
+    for k, (piece, block) in enumerate(zip(PIECES, blocks)):
+        if bits:
+            block.wait_recv()
+        else:
+            block.wait()
+        if hand_on:
+            copy = pltpu.make_async_remote_copy(
+                src_ref=part(here, piece), dst_ref=part(y_ref.at[1], piece), send_sem=h_send.at[k],
+                recv_sem=h_recv.at[k], device_id=(sibling,), device_id_type=MESH,
+            )
+            copy.start()
+            handed.append(copy)
     if bits:
-        block = pltpu.make_async_remote_copy(
-            src_ref=x_ref, dst_ref=y_ref, send_sem=x_send, recv_sem=x_recv,
-            device_id=(partner,), device_id_type=MESH,
-        )
-    else:
-        block = pltpu.make_async_copy(x_ref, y_ref, x_recv)
-    block.start()
-
-    if rounds:
-        total = s_ref[...]
-        for r, group in enumerate(peers):
-            held[r] = total
-            for k, peer in enumerate(group):
-                pltpu.make_async_remote_copy(
-                    src_ref=held.at[r], dst_ref=got[r].at[k], send_sem=s_send.at[r], recv_sem=s_recv.at[r],
-                    device_id=(peer,), device_id_type=MESH,
-                ).start()
-            pltpu.make_async_copy(got[r], got[r], s_recv.at[r]).wait()
-            total = total + jnp.sum(got[r][...], axis=0)
-        t_ref[...] = total
-        for r in range(len(rounds)):
-            pltpu.make_async_copy(got[r], got[r], s_send.at[r]).wait()
-    else:
-        t_ref[...] = s_ref[...]
-    block.wait()
-
-
-def stage_call(bits, rounds, collective_id, x, s):
+        for block in blocks:
+            block.wait_send()
+    for copy in handed:
+        copy.wait()
+
+
+def stage_call(bits, rounds, hand_on, collective_id, x, s):
     anywhere = pl.BlockSpec(memory_space=pl.ANY)
     vmem = pl.BlockSpec(memory_space=pltpu.VMEM)
+    out = ((2,) if hand_on else ()) + x.shape
+    pieces = pltpu.SemaphoreType.DMA((len(PIECES),))
+    turns = pltpu.SemaphoreType.DMA((len(rounds),))
     return pl.pallas_call(
-        functools.partial(stage_kernel, bits, rounds),
-        out_shape=(jax.ShapeDtypeStruct(x.shape, x.dtype), jax.ShapeDtypeStruct(s.shape, s.dtype)),
+        functools.partial(stage_kernel, bits, rounds, hand_on),
+        out_shape=(jax.ShapeDtypeStruct(out, x.dtype), jax.ShapeDtypeStruct(s.shape, s.dtype)),
         in_specs=[anywhere, vmem],
         out_specs=(anywhere, vmem),
         scratch_shapes=[
-            pltpu.VMEM((max(1, len(rounds)),) + s.shape, F32),
+            pltpu.VMEM((len(rounds),) + s.shape, F32),
             *[pltpu.VMEM((size - 1,) + s.shape, F32) for _, size in rounds],
-            pltpu.SemaphoreType.DMA,
-            pltpu.SemaphoreType.DMA,
-            pltpu.SemaphoreType.DMA((max(1, len(rounds)),)),
-            pltpu.SemaphoreType.DMA((max(1, len(rounds)),)),
+            pieces,
+            pieces,
+            turns,
+            turns,
+            pieces,
+            pieces,
         ],
         compiler_params=pltpu.CompilerParams(collective_id=collective_id, has_side_effects=True),
         name=f"exchange_{collective_id}",
     )(x, s)
 
 
-def stage(mask, stage_bits, rounds, first_id, x, s):
+def stage(mask, stage_bits, rounds, hand_on, first_id, x, s):
     choice = sum(jnp.bitwise_and(jnp.right_shift(mask, bit), 1) << k for k, bit in enumerate(stage_bits))
 
     def branch(value):
         bits = tuple(bit for k, bit in enumerate(stage_bits) if value >> k & 1)
-        return lambda x, s: stage_call(bits, rounds, first_id + value, x, s)
+        return lambda x, s: stage_call(bits, rounds, hand_on, first_id + value, x, s)
 
     return lax.switch(choice, [branch(value) for value in range(1 << len(stage_bits))], x, s)
 
 
 def exchange(mask, x, s):
-    x, s = stage(mask, STAGE_A, SUM_A, 0, x, s)
-    x, s = stage(mask, STAGE_B, SUM_B, 16, x, s)
-    flip = jnp.bitwise_and(jnp.right_shift(mask, CORE_BIT), 1)
-
-    def cross(x, s):
-        return stage_call((CORE_BIT,), (), 32, x, s)
-
-    return lax.cond(flip == 1, cross, lambda x, s: (x, s), x, s)
+    x, s = stage(mask, STAGE_A, SUM_A, False, 0, x, s)
+    x, s = stage(mask, STAGE_B, SUM_B, True, 16, x, s)
+    return x, jnp.bitwise_and(mask, 1), s
 
 
 def sub_epoch_kernel(
-    sub, rows, cols, counts, mean_in, totals, users_in, ubias_in, packed_in, ratings, observed,
+    sub, rows, cols, counts, place, mean_in, totals, users_in, ubias_in, pair, ratings, observed,
     users, ubias, packed, sums, mean_out,
-    ubias_wide, items_t, ibias_wide, rating_buf, seen_buf, rating_sem, seen_sem,
+    packed_in, packed_sem, users_sem, ubias_wide, items_t, ibias_wide, rating_buf, seen_buf, rating_sem, seen_sem,
 ):
     count = counts[sub]
 
@@ -144,6 +173,10 @@
             copy.start()
         return carry
 
+    arrival = pltpu.make_async_copy(pair.at[place[0]], packed_in, packed_sem)
+    arrival.start()
+    own = pltpu.make_async_copy(users_in, users, users_sem)
+    own.start()
     lax.fori_loop(0, count, start, 0)
 
     mean = mean_in[...]
@@ -159,11 +192,12 @@
         ubias_wide[a * TILE : (a + 1) * TILE, :] = jnp.broadcast_to(
             jnp.sum(across, axis=1, keepdims=True), (TILE, TILE)
         )
-        users[a * TILE : (a + 1) * TILE, :] = users_in[a * TILE : (a + 1) * TILE, :]
+    arrival.wait()
     for c in range(COL_TILES):
         items_t[c] = packed_in[c * TILE : (c + 1) * TILE, :].T
         ibias_wide[c] = jnp.broadcast_to(packed_in[ITEM_ROWS + c : ITEM_ROWS + c + 1, :], (8, TILE))
 
+    own.wait()
     learn_rate = step_scale / TILE
 
     def slot(t, carry):
@@ -209,7 +243,7 @@
     packed[ITEM_ROWS + COL_TILES : PACKED, :] = jnp.zeros((PACKED - ITEM_ROWS - COL_TILES, TILE), F32)
 
 
-def sub_epoch(sub, rows, cols, counts, mean, totals, users, ubias, packed, ratings, observed):
+def sub_epoch(sub, rows, cols, counts, place, mean, totals, users, ubias, pair, ratings, observed):
     smem = pl.BlockSpec(memory_space=pltpu.SMEM)
     vmem = pl.BlockSpec(memory_space=pltpu.VMEM)
     anywhere = pl.BlockSpec(memory_space=pl.ANY)
@@ -217,10 +251,13 @@
     shape = lambda *dims: jax.ShapeDtypeStruct(dims, F32)
     return pl.pallas_call(
         functools.partial(sub_epoch_kernel, sub),
-        out_shape=(shape(*users.shape), shape(*ubias.shape), shape(*packed.shape), shape(8, TILE), shape(1, TILE)),
-        in_specs=[smem, smem, smem, vmem, vmem, vmem, vmem, vmem, anywhere, anywhere],
+        out_shape=(shape(*users.shape), shape(*ubias.shape), shape(*pair.shape[1:]), shape(8, TILE), shape(1, TILE)),
+        in_specs=[smem, smem, smem, smem, vmem, vmem, anywhere, vmem, anywhere, anywhere, anywhere],
         out_specs=(vmem,) * 5,
         scratch_shapes=[
+            pltpu.VMEM(pair.shape[1:], F32),
+            pltpu.SemaphoreType.DMA,
+            pltpu.SemaphoreType.DMA,
             pltpu.VMEM((ROW_TILES * TILE, TILE), F32),
             pltpu.VMEM((COL_TILES, TILE, TILE), F32),
             pltpu.VMEM((COL_TILES, 8, TILE), F32),
@@ -231,7 +268,7 @@
         ],
         compiler_params=pltpu.CompilerParams(vmem_limit_bytes=24 << 20),
         name=f"sub_epoch_{sub}",
-    )(rows, cols, counts, mean, totals, users, ubias, packed, ratings, observed)
+    )(rows, cols, counts, place.reshape(1), mean, totals, users, ubias, pair, ratings, observed)
 
 
 def on_device(
@@ -253,17 +290,17 @@
     pad = jnp.zeros((PACKED - ITEM_ROWS - COL_TILES, TILE), F32)
     packed = jnp.concatenate([items, item_bias.reshape(COL_TILES, TILE), pad], axis=0)
     mean = global_mean.reshape(1, 1)
-    sums = jnp.zeros((8, TILE), F32)
-
-    packed, totals = exchange(masks[0], packed, sums)
+
+    pair, place, totals = exchange(masks[0], packed, ubias)
     users, ubias, packed, sums, mean = sub_epoch(
-        0, rows, cols, counts, mean, totals, users, ubias, packed, ratings, observed
-    )
-    packed, totals = exchange(jnp.bitwise_xor(masks[0], masks[1]), packed, sums)
+        0, rows, cols, counts, place, mean, totals, users, ubias, pair, ratings, observed
+    )
+    pair, place, totals = exchange(jnp.bitwise_xor(masks[0], masks[1]), packed, sums)
     users, ubias, packed, sums, mean = sub_epoch(
-        1, rows, cols, counts, mean[:, :1], totals, users, ubias, packed, ratings, observed
-    )
-    packed, totals = exchange(masks[1], packed, sums)
+        1, rows, cols, counts, place, mean[:, :1], totals, users, ubias, pair, ratings, observed
+    )
+    pair, place, totals = exchange(masks[1], packed, sums)
+    packed = lax.dynamic_index_in_dim(pair, place, 0, keepdims=False)
     total = jnp.sum(totals, axis=1)
     mean = mean[0, 0] + mean_rate * total[0] / total[1]
     return (

time: 179 us -> 160 us (0.89)
  Pallas kernels: 148 us -> 133 us
  local copies, waits for them, and re-layouts: 10.6 us -> 5.45 us
    pallas_call x2, Pallas kernels: 16.5 us -> 6.36 us  [sub_epoch(): pl.pallas_call(functools.partial(sub_epoch_kernel, sub), out_shape=(shape...]
    pallas_call x8 -> x6, Pallas kernels: 132 us -> 127 us  [stage_call(): pl.pallas_call(functools.partial(stage_kernel, bits, rounds, hand_on), ou...]
    cond x4 -> x0, local copies, waits for them, and re-layouts: 4.53 us -> none
where the time goes in v2:
time: 160 us; the launch traced here: 158 us
  Pallas kernels  133 us (83%)
  between operations  17 us (11%)
  local copies, waits for them, and re-layouts  5.45 us (3%)
  other arithmetic  1.87 us (1%)
    pallas_call x6, Pallas kernels, stage_call(): pl.pallas_call(functools.partial(stage_kernel, bits, rounds, hand_on), ou...  127 us
    pallas_call x2, Pallas kernels, sub_epoch(): pl.pallas_call(functools.partial(sub_epoch_kernel, sub), out_shape=(shape...  6.36 us

profile of v2, /device:TPU:1, one launch (start us, length us, event | category | flops | bytes accessed | tf_op | source)
XLA Modules:
  0.0 158.2 jit_solution(1892440660688885201)
XLA Ops:
  0.6 0.7 broadcast_xor_fusion
  1.3 0.6 fusion.1
  4.5 0.1 pad.2.clone
  4.6 1.1 maximum_maximum_fusion
  5.7 21.9 %conditional.6 = ((f32[520,128]{1,0:T(8,128)S(1)}, f32[8,128]{1,0:T(8,128)S(1)})) conditional(s32[]{:T(128)} %bitcast.7, (f32[520,128]{1,0:T(8,128)S(1)}, f32[8,128]{1,0:T(8,128)}) %tuple.446, (f32[520,128]{1,0:T(8,128)S(1)}, f32[8,128]{1,0:T(8,128)}) %tuple.447, (f32[520,128]{1,0:T(8,128)S(1)}, ...), branch_computations={%region_0.0_spmd, %region_1.0_spmd, %region_2.0_spmd, %region_3.0_... | conditional | bytes 8 | solution.py:149
  5.7 21.9 %exchange_6.3 = (f32[520,128]{1,0:T(8,128)S(1)}, f32[8,128]{1,0:T(8,128)S(1)}) custom-call(f32[520,128]{1,0:T(8,128)S(1)} %get-tuple-element.396.x_ref, f32[8,128]{1,0:T(8,128)} %get-tuple-element.397.s_ref), custom_call_target="tpu_custom_call" | custom-call | tf_op jit(solution)/shard_map/cond/branch_6_fun/exchange_6/pallas_call | solution.py:122
  30.2 0.0 copy-start
  30.2 0.0 copy-start.1
  30.2 0.0 copy-start.5
  30.2 0.0 copy-start.6
  30.2 0.0 copy-start.8
  30.3 24.2 %conditional.7 = ((f32[2,520,128]{2,1,0:T(8,128)}, f32[8,128]{1,0:T(8,128)S(1)})) conditional(s32[]{:T(128)} %bitcast.6, (f32[520,128]{1,0:T(8,128)S(1)}, f32[8,128]{1,0:T(8,128)S(1)}) %get-tuple-element.809, (f32[520,128]{1,0:T(8,128)S(1)}, f32[8,128]{1,0:T(8,128)S(1)}) %get-tuple-element.809, ...), branch_computations={%region_16.0_spmd, %region_17.0_spmd, %region_18.0_spmd, %region_1... | conditional | bytes 8 | solution.py:149
  30.3 24.1 %exchange_28.3 = (f32[2,520,128]{2,1,0:T(8,128)}, f32[8,128]{1,0:T(8,128)S(1)}) custom-call(f32[520,128]{1,0:T(8,128)S(1)} %get-tuple-element.440.x_ref, f32[8,128]{1,0:T(8,128)S(1)} %get-tuple-element.441.s_ref), custom_call_target="tpu_custom_call" | custom-call | tf_op jit(solution)/shard_map/cond/branch_12_fun/exchange_28/pallas_call | solution.py:122
  55.8 0.0 copy-start.2
  55.8 1.0 copy-done.2
  56.8 2.7 %sub_epoch_0.1 = (f32[1024,128]{1,0:T(8,128)S(1)}, f32[8,128]{1,0:T(8,128)S(1)}, f32[520,128]{1,0:T(8,128)S(1)}, f32[8,128]{1,0:T(8,128)S(1)}, f32[1,128]{1,0:T(1,128)S(1)}) custom-call(s32[2,16]{1,0:T(2,128)S(1)} %bitcast.25, s32[2,16]{1,0:T(2,128)S(1)} %bitcast.27, s32[2]{0:T(128)S(1)} %bitcast.29, s32[1]{0:T(128)} %bitcast.4.place, ...), custom_call_target="tpu_custom_call" | custom-call | tf_op jit(solution)/shard_map/sub_epoch_0/pallas_call | solution.py:252
  59.5 0.0 copy-start.3
  59.5 0.8 copy-done.3
  61.6 19.7 %conditional.8 = ((f32[520,128]{1,0:T(8,128)}, f32[8,128]{1,0:T(8,128)S(1)})) conditional(s32[]{:T(128)} %bitcast.11, (f32[520,128]{1,0:T(8,128)S(1)}, f32[8,128]{1,0:T(8,128)S(1)}) %tuple.249, (f32[520,128]{1,0:T(8,128)S(1)}, f32[8,128]{1,0:T(8,128)S(1)}) %tuple.249, (f32[520,128]{1,0:T(8,128)S(1)}, ...), branch_computations={%region_32.0_spmd, %region_33.0_spmd, %region_34.0_spmd, %region_3... | conditional | bytes 8 | solution.py:149
  61.7 19.7 %exchange_9.4 = (f32[520,128]{1,0:T(8,128)}, f32[8,128]{1,0:T(8,128)S(1)}) custom-call(f32[520,128]{1,0:T(8,128)S(1)} %get-tuple-element.466.x_ref, f32[8,128]{1,0:T(8,128)S(1)} %get-tuple-element.467.s_ref), custom_call_target="tpu_custom_call" | custom-call | tf_op jit(solution)/shard_map/cond/branch_9_fun/exchange_9/pallas_call | solution.py:122
  81.4 18.0 %conditional.9 = ((f32[2,520,128]{2,1,0:T(8,128)}, f32[8,128]{1,0:T(8,128)S(1)})) conditional(s32[]{:T(128)} %bitcast.10, (f32[520,128]{1,0:T(8,128)}, f32[8,128]{1,0:T(8,128)S(1)}) %get-tuple-element.811, (f32[520,128]{1,0:T(8,128)}, f32[8,128]{1,0:T(8,128)S(1)}) %get-tuple-element.811, (f32[520,128]{1,0:T(8,128)}, ...), branch_computations={%region_48.0_spmd, %region_49.0_spmd, %region_50.0_spmd, %region_5... | conditional | bytes 8 | solution.py:149
  81.6 17.7 %exchange_27.4 = (f32[2,520,128]{2,1,0:T(8,128)}, f32[8,128]{1,0:T(8,128)S(1)}) custom-call(f32[520,128]{1,0:T(8,128)} %get-tuple-element.502.x_ref, f32[8,128]{1,0:T(8,128)S(1)} %get-tuple-element.503.s_ref), custom_call_target="tpu_custom_call" | custom-call | tf_op jit(solution)/shard_map/cond/branch_11_fun/exchange_27/pallas_call | solution.py:122
  99.4 1.0 copy-done.4
  100.4 3.7 %sub_epoch_1.1 = (f32[1024,128]{1,0:T(8,128)}, f32[8,128]{1,0:T(8,128)}, f32[520,128]{1,0:T(8,128)S(1)}, f32[8,128]{1,0:T(8,128)S(1)}, f32[1,128]{1,0:T(1,128)S(1)}) custom-call(s32[2,16]{1,0:T(2,128)S(1)} %bitcast.26, s32[2,16]{1,0:T(2,128)S(1)} %bitcast.28, s32[2]{0:T(128)S(1)} %bitcast.30, s32[1]{0:T(128)} %bitcast.3.place, f32[1,1]{1,0:T(1,128)S(1)} %bitcast.31, ...), custom_call_target="tpu_custom_call" | custom-call | tf_op jit(solution)/shard_map/sub_epoch_1/pallas_call | solution.py:252
  106.7 24.4 %conditional.10 = ((f32[520,128]{1,0:T(8,128)S(1)}, f32[8,128]{1,0:T(8,128)S(1)})) conditional(s32[]{:T(128)} %bitcast.14, (f32[520,128]{1,0:T(8,128)S(1)}, f32[8,128]{1,0:T(8,128)S(1)}) %tuple.250, (f32[520,128]{1,0:T(8,128)S(1)}, f32[8,128]{1,0:T(8,128)S(1)}) %tuple.250, (f32[520,128]{1,0:T(8,128)S(1)}, ...), branch_computations={%region_64.0_spmd, %region_65.0_spmd, %region_66.0_spmd, %region_6... | conditional | bytes 8 | solution.py:149
  106.7 24.4 %exchange_15.5 = (f32[520,128]{1,0:T(8,128)S(1)}, f32[8,128]{1,0:T(8,128)S(1)}) custom-call(f32[520,128]{1,0:T(8,128)S(1)} %get-tuple-element.542.x_ref, f32[8,128]{1,0:T(8,128)S(1)} %get-tuple-element.543.s_ref), custom_call_target="tpu_custom_call" | custom-call | tf_op jit(solution)/shard_map/cond/branch_15_fun/exchange_15/pallas_call | solution.py:122
  133.7 19.3 %conditional.11 = ((f32[2,520,128]{2,1,0:T(8,128)S(1)}, f32[8,128]{1,0:T(8,128)S(1)})) conditional(s32[]{:T(128)} %bitcast.13, (f32[520,128]{1,0:T(8,128)S(1)}, f32[8,128]{1,0:T(8,128)S(1)}) %get-tuple-element.813, (f32[520,128]{1,0:T(8,128)S(1)}, f32[8,128]{1,0:T(8,128)S(1)}) %get-tuple-element.813, ...), branch_computations={%region_80.0_spmd, %region_81.0_spmd, %region_82.0_spmd, %region_8... | conditional | bytes 8 | solution.py:149
  133.8 19.3 %exchange_23.5 = (f32[2,520,128]{2,1,0:T(8,128)S(1)}, f32[8,128]{1,0:T(8,128)S(1)}) custom-call(f32[520,128]{1,0:T(8,128)S(1)} %get-tuple-element.558.x_ref, f32[8,128]{1,0:T(8,128)S(1)} %get-tuple-element.559.s_ref), custom_call_target="tpu_custom_call" | custom-call | tf_op jit(solution)/shard_map/cond/branch_7_fun/exchange_23/pallas_call | solution.py:122
  153.0 0.1 reduce_sum.9
  153.1 0.6 fusion
  155.8 0.7 dynamic-slice_bitcast_fusion
  156.5 0.6 dynamic-slice_bitcast_fusion.1
  (9 shorter events, 0.0 us)
Async XLA Ops:
  30.2 25.5 %copy-start = (s32[2,1,16,128,128]{4,3,2,1,0:T(8,128)S(1)}, s32[2,1,16,128,128]{4,3,2,1,0:T(8,128)}, u32[]{:S(2)}) copy-start(s32[2,1,16,128,128]{4,3,2,1,0:T(8,128)} %observed.3) | copy-start | bytes 6291460
  30.2 25.5 %copy-start.1 = (bf16[2,1,16,128,128]{4,3,2,1,0:T(8,128)(2,1)S(1)}, bf16[2,1,16,128,128]{4,3,2,1,0:T(8,128)(2,1)}, u32[]{:S(2)}) copy-start(bf16[2,1,16,128,128]{4,3,2,1,0:T(8,128)(2,1)} %ratings.3) | copy-start | bytes 3145732
  30.2 25.5 %copy-start.5 = (s32[2,1,16]{2,1,0:T(1,128)S(1)}, s32[2,1,16]{2,1,0:T(1,128)}, u32[]{:S(2)}) copy-start(s32[2,1,16]{2,1,0:T(1,128)} %param.113) | copy-start | bytes 388
  30.2 25.5 %copy-start.6 = (s32[2,1,16]{2,1,0:T(1,128)S(1)}, s32[2,1,16]{2,1,0:T(1,128)}, u32[]{:S(2)}) copy-start(s32[2,1,16]{2,1,0:T(1,128)} %param.114) | copy-start | bytes 388
  30.2 25.5 %copy-start.7 = (s32[2,1]{0,1:T(1,128)S(1)}, s32[2,1]{0,1:T(1,128)}, u32[]{:S(2)}) copy-start(s32[2,1]{0,1:T(1,128)} %param.115) | copy-start | bytes 28
  30.2 25.5 %copy-start.8 = (f32[1024]{0:T(1024)S(1)}, f32[1024]{0:T(1024)}, u32[]{:S(2)}) copy-start(f32[1024]{0:T(1024)} %param.108) | copy-start | bytes 12292
  55.8 1.0 copy-start.2
  59.5 0.8 copy-start.3
  99.4 1.0 copy-start.4
